TPU v7x, 32 devices: a whole 2x2x4 slice. The times are simulated.
32 devices in a mesh: dom: 8 (over z, y), feat: 4 (over x, core).
Axes of the slice: x: 2, y: 2, z: 4, core: 2. Of those that a mesh axis runs over, the one named last changes fastest.
Arguments:
- features: bfloat16 [3584, 128], P('dom'), may hold values from -6 to 6
- perturb: bfloat16 [3584, 128], P('dom'), may hold values from -0.5 to 0.5
- w_self: bfloat16 [128, 1024], P(None, 'feat'), may hold values from -0.5 to 0.5
- w_neigh: bfloat16 [128, 1024], P(None, 'feat'), may hold values from -0.5 to 0.5
- bias: float32 [1024], P('feat'), may hold values from -3 to 3
- upstream: bfloat16 [3584, 1024], P('dom', 'feat'), may hold values from -0.09375 to 0.09375
- hub_rows: int32 [8, 2], P('dom'), may hold values from 0 to 447, as said below
- send_rows: int32 [8, 4, 56], P('dom'), may hold values from -1 to 447, as said below
- neighbors: int32 [3584, 15], P('dom'), may hold values from 0 to 687, as said below
Outputs:
- new_perturb: bfloat16 [3584, 128], P('dom', 'feat')
- grad_self: float32 [128, 1024], P(None, 'feat')
- grad_neigh: float32 [128, 1024], P(None, 'feat')
Inputs may be any that keep to these rules, and one draw needn't show every extreme that they name: hub_rows[s] are distinct rows of partition s. send_rows[s, o] lists distinct rows of partition s sent to partition s + off(o) mod 8; live entries come first, at least 14 of them, and in every draw some list is full with 56 live entries. `neighbors`: indices below 448 are rows of the node's own partition; indices 448 + o * 56 + j refer only to live slots of the list that partition s = p - off(o) mod 8 sends to p; indices from 672 on are hub nodes.
All inputs are finite; a program needn't handle non-finite values.
Results may differ from a plain program's by a relative error of at most 0.001.
The roundings to bfloat16 on the way count: a program that leaves them out, or rounds other values in their place, can miss the bound.
Values may be sent and summed in bfloat16 or wider, within the bound.
A program may use at most 64 MiB of HBM per device.

v0:
```python
import functools

import jax
import jax.numpy as jnp
from jax import lax
from jax.experimental import pallas as pl
from jax.experimental.pallas import tpu as pltpu
from jax.sharding import PartitionSpec as P

K = 15
NOFF = 4
HUB_SLOT = 8
ROW_TILE = 16
BUILD = 32
MESH = pl.DeviceIdType.MESH
F32 = jnp.float32
BF16 = jnp.bfloat16


def offset_of(direction):
    return direction - 2 if direction < 2 else direction - 1


def dot(left, right, dims):
    return lax.dot_general(left, right, (dims, ((), ())), preferred_element_type=F32)


NN = ((1,), (0,))
NT = ((1,), (1,))


def halves(value, axis):
    high = value.astype(BF16)
    low = (value - high.astype(F32)).astype(BF16)
    return jnp.concatenate([high, low], axis)


def each(count, body):
    if count <= 8:
        for step in range(count):
            body(step)
    else:

        def run(step, carry):
            body(step)
            return carry

        lax.fori_loop(0, count, run, 0)


def kernel(
    doms,
    feats,
    owners,
    slots,
    features,
    perturb,
    w_self,
    w_neigh,
    bias,
    upstream,
    hub_rows,
    send_rows,
    neighbors,
    new_perturb,
    grad_self,
    grad_neigh,
    lists,
    counts,
    perturb_t,
    halo_out,
    halo_in,
    hub_out,
    hub_in,
    back_out,
    back_in,
    hubg_out,
    hubg_in,
    part_out,
    part_in,
    whole,
    cols_out,
    cols_in,
    sq_out,
    sq_in,
    halo_s,
    halo_r,
    hub_s,
    hub_r,
    back_s,
    back_r,
    hubg_s,
    hubg_r,
    part_s,
    part_r,
    whole_s,
    whole_r,
    cols_s,
    cols_r,
    sq_s,
    sq_r,
):
    me = lax.axis_index("dom")
    col = lax.axis_index("feat")
    rows, width = features.shape
    slot_pad = halo_out.shape[1]
    halo_rows = NOFF * slot_pad
    chunk = part_out.shape[1]

    def dom_peer(step):
        return lax.rem(me + step + 1, doms)

    def feat_peer(step):
        return lax.rem(col + step + 1, feats)

    def at_offset(by):
        return lax.rem(me + by + doms, doms)

    barrier = pltpu.get_barrier_semaphore()

    def greet_dom(step):
        pl.semaphore_signal(
            barrier, inc=1, device_id=(dom_peer(step), col), device_id_type=MESH
        )

    def greet_feat(step):
        pl.semaphore_signal(
            barrier, inc=1, device_id=(me, feat_peer(step)), device_id_type=MESH
        )

    each(doms - 1, greet_dom)
    each(feats - 1, greet_feat)

    def copy_to(src, dst, send, recv, dom, feat):
        return pltpu.make_async_remote_copy(
            src_ref=src,
            dst_ref=dst,
            send_sem=send,
            recv_sem=recv,
            device_id=(dom, feat),
            device_id_type=MESH,
        )

    perturb_f32 = perturb[...].astype(F32)
    perturbed = (features[...].astype(F32) + perturb_f32).astype(BF16)
    lists[...] = jnp.full(lists.shape, -1, jnp.int32)
    lists[0:NOFF, 0:slots] = send_rows[0]
    lists[NOFF : NOFF + 1, 0 : hub_rows.shape[1]] = hub_rows[...]
    by_slot = jnp.transpose(lists[...].astype(F32))
    row_ids = lax.broadcasted_iota(jnp.int32, (slot_pad, rows), 1).astype(F32)
    picks = [
        jnp.where(by_slot[0:slot_pad, o : o + 1] == row_ids, 1.0, 0.0).astype(BF16)
        for o in range(NOFF)
    ]
    pick_halo = jnp.concatenate(picks, 0)
    pick_hub = jnp.where(
        by_slot[0:ROW_TILE, NOFF : NOFF + 1] == row_ids[0:ROW_TILE], 1.0, 0.0
    ).astype(BF16)
    picked = dot(pick_halo, perturbed, NN).astype(BF16)
    for o in range(NOFF):
        halo_out[o] = picked[o * slot_pad : (o + 1) * slot_pad]
    own_hubs = dot(pick_hub, perturbed, NN)[0:HUB_SLOT]
    hub_out[...] = own_hubs
    hub_in[me] = own_hubs

    pl.semaphore_wait(barrier, doms - 1 + feats - 1)

    def halo_copy(o):
        return copy_to(
            halo_out.at[o], halo_in.at[o], halo_s.at[o], halo_r.at[o], at_offset(offset_of(o)), col
        )

    def hub_send(step):
        peer = dom_peer(step)
        return copy_to(hub_out, hub_in.at[me], hub_s.at[peer], hub_r.at[me], peer, col)

    def hub_recv(step):
        peer = dom_peer(step)
        return copy_to(hub_out, hub_in.at[peer], hub_s.at[peer], hub_r.at[peer], peer, col)

    for o in range(NOFF):
        halo_copy(o).start()
    each(doms - 1, lambda step: hub_send(step).start())

    nodes = neighbors[...]
    far = nodes - rows
    shifted = nodes
    for o in range(1, NOFF):
        shifted = shifted + jnp.where(far >= o * slots, slot_pad - slots, 0)
    hub_id = far - NOFF * slots
    hub_at = rows + halo_rows + (hub_id >> 1) * HUB_SLOT + (hub_id & 1)
    place = jnp.where(hub_id >= 0, hub_at, shifted)

    def build(block, carry):
        first = pl.multiple_of(block * BUILD, BUILD)
        ids = lax.broadcasted_iota(jnp.int32, (BUILD, rows), 0) + first
        total = jnp.zeros((BUILD, rows), F32)
        for k in range(K):
            total = total + jnp.where(place[k : k + 1] == ids, 1.0, 0.0)
        counts[pl.ds(first, BUILD)] = total.astype(BF16)
        return carry

    lax.fori_loop(0, counts.shape[0] // BUILD, build, 0)

    turned = jnp.transpose(perturb_f32)
    for g in range(feats):
        perturb_t[g] = turned[g * (width // feats) : (g + 1) * (width // feats)]
    perturbed_t = jnp.transpose(perturbed.astype(F32)).astype(BF16)
    summed_t = dot(perturbed_t, counts[0:rows], NN)
    preact_self = dot(perturbed, w_self[...], NN) + bias[...]

    for o in range(NOFF):
        halo_copy(o).wait_recv()
    each(doms - 1, lambda step: hub_recv(step).wait_recv())
    remote = jnp.concatenate(
        [halo_in[...].astype(F32).reshape(halo_rows, width), hub_in[...].reshape(-1, width)], 0
    )
    remote_t = jnp.transpose(remote).astype(BF16)
    summed_t = summed_t + dot(remote_t, counts[rows:], NN)
    mean_t = summed_t / K
    mean = jnp.transpose(mean_t).astype(BF16)
    preact = preact_self + dot(mean, w_neigh[...], NN)
    sigmoid_pre = jax.nn.sigmoid(preact)
    grad_pre = (
        upstream[...].astype(F32) * sigmoid_pre * (1.0 + preact * (1.0 - sigmoid_pre))
    ).astype(BF16)

    spread_t = halves(dot(w_neigh[...], grad_pre, NT) / K, 0)
    back = dot(counts[rows:], spread_t, NT)
    back = back[:, 0:width] + back[:, width:]
    for o in range(NOFF):
        back_out[o] = back[o * slot_pad : (o + 1) * slot_pad]
    hubg_out[...] = back[halo_rows:].reshape(hubg_out.shape)

    def back_copy(o):
        return copy_to(
            back_out.at[o], back_in.at[o], back_s.at[o], back_r.at[o], at_offset(-offset_of(o)), col
        )

    def hubg_send(step):
        peer = dom_peer(step)
        return copy_to(
            hubg_out.at[peer], hubg_in.at[me], hubg_s.at[peer], hubg_r.at[me], peer, col
        )

    def hubg_recv(step):
        peer = dom_peer(step)
        return copy_to(
            hubg_out.at[peer], hubg_in.at[peer], hubg_s.at[peer], hubg_r.at[peer], peer, col
        )

    for o in range(NOFF):
        back_copy(o).start()
    each(doms - 1, lambda step: hubg_send(step).start())

    both_t = jnp.concatenate([perturbed_t, mean_t.astype(BF16)], 0)
    weight_grads = dot(both_t, grad_pre, NN)
    for i in range(owners):
        part_out[i] = weight_grads[i * chunk : (i + 1) * chunk]

    def on_owner(dom, body):
        if owners == doms:
            body()
        else:
            pl.when(dom < owners)(body)

    def part_send(step):
        peer = dom_peer(step)
        return copy_to(part_out.at[peer], part_in.at[me], part_s.at[peer], part_r.at[me], peer, col)

    def part_recv(step):
        peer = dom_peer(step)
        return copy_to(part_out.at[0], part_in.at[peer], part_s.at[peer], part_r.at[peer], peer, col)

    def whole_send(step):
        peer = dom_peer(step)
        return copy_to(whole.at[me], whole.at[me], whole_s.at[peer], whole_r.at[me], peer, col)

    def whole_recv(step):
        peer = dom_peer(step)
        return copy_to(whole.at[peer], whole.at[peer], whole_s.at[peer], whole_r.at[peer], peer, col)

    each(doms - 1, lambda step: on_owner(dom_peer(step), lambda: part_send(step).start()))

    local = dot(spread_t, counts[0:rows], NT)
    grad_t = dot(w_self[...], grad_pre, NT) + local[0:width] + local[width:]

    for o in range(NOFF):
        back_copy(o).wait_recv()
    each(doms - 1, lambda step: hubg_recv(step).wait_recv())
    hubg_in[me] = hubg_out[me]
    hub_sum = jnp.sum(hubg_in[...], 0)
    hub_sum = jnp.concatenate([hub_sum, jnp.zeros((ROW_TILE - HUB_SLOT, width), F32)], 0)
    returned_t = halves(jnp.transpose(back_in[...].reshape(halo_rows, width)), 0)
    hub_sum_t = halves(jnp.transpose(hub_sum), 0)
    added = dot(returned_t, pick_halo, NN) + dot(hub_sum_t, pick_hub, NN)
    grad_t = grad_t + added[0:width] + added[width:]
    part_width = width // feats
    for g in range(feats):
        cols_out[g] = grad_t[g * part_width : (g + 1) * part_width]

    def cols_send(step):
        peer = feat_peer(step)
        return copy_to(cols_out.at[peer], cols_in.at[col], cols_s.at[peer], cols_r.at[col], me, peer)

    def cols_recv(step):
        peer = feat_peer(step)
        return copy_to(
            cols_out.at[peer], cols_in.at[peer], cols_s.at[peer], cols_r.at[peer], me, peer
        )

    each(feats - 1, lambda step: cols_send(step).start())

    def sum_parts():
        each(doms - 1, lambda step: part_recv(step).wait_recv())
        part_in[me] = part_out[me]
        whole[me] = jnp.sum(part_in[...], 0)
        each(doms - 1, lambda step: whole_send(step).start())

    on_owner(me, sum_parts)

    each(feats - 1, lambda step: cols_recv(step).wait_recv())
    cols_in[col] = cols_out[col]
    grad_cols = jnp.sum(cols_in[...], 0)
    square = jnp.sum(grad_cols * grad_cols, 0, keepdims=True)
    sq_out[...] = jnp.broadcast_to(square, sq_out.shape)

    def sq_send(step):
        peer = feat_peer(step)
        return copy_to(sq_out, sq_in.at[col], sq_s.at[peer], sq_r.at[col], me, peer)

    def sq_recv(step):
        peer = feat_peer(step)
        return copy_to(sq_out, sq_in.at[peer], sq_s.at[peer], sq_r.at[peer], me, peer)

    each(feats - 1, lambda step: sq_send(step).start())
    each(feats - 1, lambda step: sq_recv(step).wait_recv())
    sq_in[col] = sq_out[...]
    mean_square = jnp.sum(sq_in[...], 0)[0:1] / width
    stepped = perturb_t[col] + 0.5 * grad_cols / jnp.sqrt(mean_square + 1e-06)
    finish(new_perturb, stepped)

    def take_whole(step):
        on_owner(dom_peer(step), lambda: whole_recv(step).wait_recv())

    each(doms - 1, take_whole)
    half = owners // 2
    grad_self[...] = whole[0:half].reshape(grad_self.shape)
    grad_neigh[...] = whole[half:owners].reshape(grad_neigh.shape)

    for o in range(NOFF):
        halo_copy(o).wait_send()
        back_copy(o).wait_send()
    each(doms - 1, lambda step: hub_send(step).wait_send())
    each(doms - 1, lambda step: hubg_send(step).wait_send())
    each(doms - 1, lambda step: on_owner(dom_peer(step), lambda: part_send(step).wait_send()))
    on_owner(me, lambda: each(doms - 1, lambda step: whole_send(step).wait_send()))
    each(feats - 1, lambda step: cols_send(step).wait_send())
    each(feats - 1, lambda step: sq_send(step).wait_send())


def finish(new_perturb, stepped):
    new_perturb[...] = stepped.astype(BF16)


def per_device(
    doms, feats, features, perturb, w_self, w_neigh, bias, upstream, hub_rows, send_rows, neighbors
):
    rows, width = features.shape
    hidden = w_self.shape[1]
    slots = send_rows.shape[2]
    slot_pad = (slots + ROW_TILE - 1) // ROW_TILE * ROW_TILE
    chunk = max(8, 2 * width // doms)
    owners = 2 * width // chunk
    table = rows + NOFF * slot_pad + doms * HUB_SLOT
    part_width = width // feats
    vmem = pl.BlockSpec(memory_space=pltpu.VMEM)
    sems = pltpu.SemaphoreType.DMA
    scratch = [
        pltpu.VMEM((8, 128), jnp.int32),
        pltpu.VMEM((table, rows), BF16),
        pltpu.VMEM((feats, part_width, rows), F32),
        pltpu.VMEM((NOFF, slot_pad, width), BF16),
        pltpu.VMEM((NOFF, slot_pad, width), BF16),
        pltpu.VMEM((HUB_SLOT, width), F32),
        pltpu.VMEM((doms, HUB_SLOT, width), F32),
        pltpu.VMEM((NOFF, slot_pad, width), F32),
        pltpu.VMEM((NOFF, slot_pad, width), F32),
        pltpu.VMEM((doms, HUB_SLOT, width), F32),
        pltpu.VMEM((doms, HUB_SLOT, width), F32),
        pltpu.VMEM((owners, chunk, hidden), F32),
        pltpu.VMEM((doms, chunk, hidden), F32),
        pltpu.VMEM((owners, chunk, hidden), F32),
        pltpu.VMEM((feats, part_width, rows), F32),
        pltpu.VMEM((feats, part_width, rows), F32),
        pltpu.VMEM((8, rows), F32),
        pltpu.VMEM((feats, 8, rows), F32),
        sems((NOFF,)),
        sems((NOFF,)),
        sems((doms,)),
        sems((doms,)),
        sems((NOFF,)),
        sems((NOFF,)),
        sems((doms,)),
        sems((doms,)),
        sems((doms,)),
        sems((doms,)),
        sems((doms,)),
        sems((doms,)),
        sems((feats,)),
        sems((feats,)),
        sems((feats,)),
        sems((feats,)),
    ]
    new_t, grad_self, grad_neigh = pl.pallas_call(
        functools.partial(kernel, doms, feats, owners, slots),
        out_shape=(
            jax.ShapeDtypeStruct((part_width, rows), BF16),
            jax.ShapeDtypeStruct((width, hidden), F32),
            jax.ShapeDtypeStruct((width, hidden), F32),
        ),
        in_specs=[vmem] * 9,
        out_specs=(vmem,) * 3,
        scratch_shapes=scratch,
        compiler_params=pltpu.CompilerParams(
            collective_id=0, has_side_effects=True, vmem_limit_bytes=40 * 2**20
        ),
    )(
        features,
        perturb,
        w_self,
        w_neigh,
        bias.reshape(1, hidden),
        upstream,
        hub_rows,
        send_rows,
        neighbors.T,
    )
    return new_t.T, grad_self, grad_neigh


def solution(mesh):
    in_specs = (
        P("dom", None),
        P("dom", None),
        P(None, "feat"),
        P(None, "feat"),
        P("feat"),
        P("dom", "feat"),
        P("dom", None),
        P("dom", None, None),
        P("dom", None),
    )
    out_specs = (P("dom", "feat"), P(None, "feat"), P(None, "feat"))
    return jax.shard_map(
        functools.partial(per_device, mesh.shape["dom"], mesh.shape["feat"]),
        mesh=mesh,
        in_specs=in_specs,
        out_specs=out_specs,
        check_vma=False,
    )
```

profile of v0, /device:TPU:0, one launch (start us, length us, event | category | flops | bytes accessed | tf_op | source)
XLA Modules:
  0.0 36.4 jit_solution(11578270433074402712)
XLA Ops:
  0.6 0.0 copy-start.6
  0.6 0.0 copy-start.7
  0.7 0.0 copy-start.8
  0.7 0.7 %copy-done.6 = s32[1,4,56]{2,1,0:T(4,128)S(1)} copy-done((s32[1,4,56]{2,1,0:T(4,128)S(1)}, s32[1,4,56]{2,1,0:T(4,128)}, u32[]{:S(2)}) %copy-start.6) | copy-done | bytes 920
  1.3 0.0 copy-done.7
  1.3 0.0 copy-done.8
  1.3 0.0 copy-start
  1.3 0.9 %copy-done = bf16[448,256]{1,0:T(8,128)(2,1)S(1)} copy-done((bf16[448,256]{1,0:T(8,128)(2,1)S(1)}, bf16[448,256]{1,0:T(8,128)(2,1)}, u32[]{:S(2)}) %copy-start) | copy-done | bytes 229400
  2.3 0.0 copy-start.1
  2.3 0.9 %copy-done.1 = bf16[448,128]{1,0:T(8,128)(2,1)S(1)} copy-done((bf16[448,128]{1,0:T(8,128)(2,1)S(1)}, bf16[448,128]{1,0:T(8,128)(2,1)}, u32[]{:S(2)}) %copy-start.1) | copy-done | bytes 114712
  3.2 0.0 copy-start.2
  3.2 0.9 %copy-done.2 = bf16[448,128]{1,0:T(8,128)(2,1)S(1)} copy-done((bf16[448,128]{1,0:T(8,128)(2,1)S(1)}, bf16[448,128]{1,0:T(8,128)(2,1)}, u32[]{:S(2)}) %copy-start.2) | copy-done | bytes 114712
  4.1 0.0 copy-start.3
  4.1 0.8 %copy-done.3 = bf16[128,256]{1,0:T(8,128)(2,1)S(1)} copy-done((bf16[128,256]{1,0:T(8,128)(2,1)S(1)}, bf16[128,256]{1,0:T(8,128)(2,1)}, u32[]{:S(2)}) %copy-start.3) | copy-done | bytes 65560
  4.9 0.0 copy-start.4
  4.9 0.8 %copy-done.4 = bf16[128,256]{1,0:T(8,128)(2,1)S(1)} copy-done((bf16[128,256]{1,0:T(8,128)(2,1)S(1)}, bf16[128,256]{1,0:T(8,128)(2,1)}, u32[]{:S(2)}) %copy-start.4) | copy-done | bytes 65560
  5.7 0.0 copy-start.5
  5.8 0.8 %copy-done.5 = s32[448,15]{0,1:T(8,128)S(1)} copy-done((s32[448,15]{0,1:T(8,128)S(1)}, s32[448,15]{0,1:T(8,128)}, u32[]{:S(2)}) %copy-start.5) | copy-done | bytes 26904
  6.5 27.9 %shard_map.112 = (bf16[32,448]{1,0:T(8,128)(2,1)S(1)}, f32[128,256]{1,0:T(8,128)S(1)}, f32[128,256]{1,0:T(8,128)S(1)}) custom-call(bf16[448,128]{1,0:T(8,128)(2,1)S(1)} %copy-done.1, bf16[448,128]{1,0:T(8,128)(2,1)S(1)} %copy-done.2, bf16[128,256]{1,0:T(8,128)(2,1)S(1)} %copy-done.3, bf16[128,256]{1,0:T(8,128)(2,1)S(1)} %copy-done.4, f32[1,256]{1,0:T(1,128)S(1)} %bitcast.5, ...), custom_call_target="tpu_custom_call" | custom-call | tf_op jit(solution)/shard_map/pallas_call | solution.py:415
  34.4 0.6 %copy.15 = bf16[448,32]{0,1:T(8,128)(2,1)} copy(bf16[448,32]{0,1:T(8,128)(2,1)S(1)} %bitcast.4) | data formatting | bytes 57344
  35.0 0.7 %copy.16 = f32[128,256]{1,0:T(8,128)} copy(f32[128,256]{1,0:T(8,128)S(1)} %get-tuple-element.13) | data formatting | bytes 262144
  35.7 0.7 %copy.17 = f32[128,256]{1,0:T(8,128)} copy(f32[128,256]{1,0:T(8,128)S(1)} %get-tuple-element.14) | data formatting | bytes 262144
Async XLA Ops:
  0.6 0.7 %copy-start.6 = (s32[1,4,56]{2,1,0:T(4,128)S(1)}, s32[1,4,56]{2,1,0:T(4,128)}, u32[]{:S(2)}) copy-start(s32[1,4,56]{2,1,0:T(4,128)} %send_rows.1) | copy-start | bytes 2692
  0.6 0.7 %copy-start.7 = (f32[256]{0:T(256)S(1)}, f32[256]{0:T(256)}, u32[]{:S(2)}) copy-start(f32[256]{0:T(256)} %param.13) | copy-start | bytes 3076
  0.7 0.7 %copy-start.8 = (s32[1,2]{1,0:T(1,128)S(1)}, s32[1,2]{1,0:T(1,128)}, u32[]{:S(2)}) copy-start(s32[1,2]{1,0:T(1,128)} %hub_rows.1) | copy-start | bytes 28
  1.3 0.9 %copy-start = (bf16[448,256]{1,0:T(8,128)(2,1)S(1)}, bf16[448,256]{1,0:T(8,128)(2,1)}, u32[]{:S(2)}) copy-start(bf16[448,256]{1,0:T(8,128)(2,1)} %upstream.1) | copy-start | bytes 688132
  2.3 0.9 %copy-start.1 = (bf16[448,128]{1,0:T(8,128)(2,1)S(1)}, bf16[448,128]{1,0:T(8,128)(2,1)}, u32[]{:S(2)}) copy-start(bf16[448,128]{1,0:T(8,128)(2,1)} %features.1) | copy-start | bytes 344068
  3.2 0.9 %copy-start.2 = (bf16[448,128]{1,0:T(8,128)(2,1)S(1)}, bf16[448,128]{1,0:T(8,128)(2,1)}, u32[]{:S(2)}) copy-start(bf16[448,128]{1,0:T(8,128)(2,1)} %perturb.1) | copy-start | bytes 344068
  4.1 0.8 %copy-start.3 = (bf16[128,256]{1,0:T(8,128)(2,1)S(1)}, bf16[128,256]{1,0:T(8,128)(2,1)}, u32[]{:S(2)}) copy-start(bf16[128,256]{1,0:T(8,128)(2,1)} %w_self.1) | copy-start | bytes 196612
  4.9 0.8 %copy-start.4 = (bf16[128,256]{1,0:T(8,128)(2,1)S(1)}, bf16[128,256]{1,0:T(8,128)(2,1)}, u32[]{:S(2)}) copy-start(bf16[128,256]{1,0:T(8,128)(2,1)} %w_neigh.1) | copy-start | bytes 196612
  5.7 0.8 %copy-start.5 = (s32[448,15]{0,1:T(8,128)S(1)}, s32[448,15]{0,1:T(8,128)}, u32[]{:S(2)}) copy-start(s32[448,15]{0,1:T(8,128)} %param.17) | copy-start | bytes 80644
where the time goes:
time: 36.7 us; the launch traced here: 36.4 us
  Pallas kernels  27.9 us (76%)
  local copies, waits for them, and re-layouts  7.77 us (21%)
  between operations  0.67 us (2%)
    pallas_call x1, Pallas kernels, per_device(): pl.pallas_call(functools.partial(kernel, doms, feats, owners, slots), out...  27.9 us
    unnamed x21, local copies, waits for them, and re-layouts  7.77 us

commit v1 on v0

--- a/solution.py
+++ b/solution.py
@@ -53,15 +53,15 @@
     feats,
     owners,
     slots,
-    features,
-    perturb,
-    w_self,
-    w_neigh,
-    bias,
-    upstream,
-    hub_rows,
-    send_rows,
-    neighbors,
+    features_far,
+    perturb_far,
+    send_rows_far,
+    hub_rows_far,
+    neighbors_far,
+    w_self_far,
+    bias_far,
+    w_neigh_far,
+    upstream_far,
     new_perturb,
     grad_self,
     grad_neigh,
@@ -99,7 +99,35 @@
     cols_r,
     sq_s,
     sq_r,
+    features,
+    perturb,
+    send_rows,
+    hub_rows,
+    neighbors,
+    w_self,
+    bias,
+    w_neigh,
+    upstream,
+    load_s,
 ):
+    far = (
+        features_far,
+        perturb_far,
+        send_rows_far,
+        hub_rows_far,
+        neighbors_far,
+        w_self_far,
+        bias_far,
+        w_neigh_far,
+        upstream_far,
+    )
+    near = (features, perturb, send_rows, hub_rows, neighbors, w_self, bias, w_neigh, upstream)
+    loads = [
+        pltpu.make_async_copy(there, here, load_s.at[i])
+        for i, (there, here) in enumerate(zip(far, near))
+    ]
+    for load in loads:
+        load.start()
     me = lax.axis_index("dom")
     col = lax.axis_index("feat")
     rows, width = features.shape
@@ -141,6 +169,8 @@
             device_id_type=MESH,
         )
 
+    for load in loads[0:4]:
+        load.wait()
     perturb_f32 = perturb[...].astype(F32)
     perturbed = (features[...].astype(F32) + perturb_f32).astype(BF16)
     lists[...] = jnp.full(lists.shape, -1, jnp.int32)
@@ -182,12 +212,14 @@
         halo_copy(o).start()
     each(doms - 1, lambda step: hub_send(step).start())
 
+    for load in loads[4:7]:
+        load.wait()
     nodes = neighbors[...]
-    far = nodes - rows
+    beyond = nodes - rows
     shifted = nodes
     for o in range(1, NOFF):
-        shifted = shifted + jnp.where(far >= o * slots, slot_pad - slots, 0)
-    hub_id = far - NOFF * slots
+        shifted = shifted + jnp.where(beyond >= o * slots, slot_pad - slots, 0)
+    hub_id = beyond - NOFF * slots
     hub_at = rows + halo_rows + (hub_id >> 1) * HUB_SLOT + (hub_id & 1)
     place = jnp.where(hub_id >= 0, hub_at, shifted)
 
@@ -209,6 +241,8 @@
     summed_t = dot(perturbed_t, counts[0:rows], NN)
     preact_self = dot(perturbed, w_self[...], NN) + bias[...]
 
+    for load in loads[7:9]:
+        load.wait()
     for o in range(NOFF):
         halo_copy(o).wait_recv()
     each(doms - 1, lambda step: hub_recv(step).wait_recv())
@@ -374,6 +408,7 @@
     owners = 2 * width // chunk
     table = rows + NOFF * slot_pad + doms * HUB_SLOT
     part_width = width // feats
+    hbm = pl.BlockSpec(memory_space=pltpu.HBM)
     vmem = pl.BlockSpec(memory_space=pltpu.VMEM)
     sems = pltpu.SemaphoreType.DMA
     scratch = [
@@ -412,6 +447,18 @@
         sems((feats,)),
         sems((feats,)),
     ]
+    args = (
+        features,
+        perturb,
+        send_rows,
+        hub_rows,
+        neighbors.T,
+        w_self,
+        bias.reshape(1, hidden),
+        w_neigh,
+        upstream,
+    )
+    scratch += [pltpu.VMEM(x.shape, x.dtype) for x in args] + [sems((len(args),))]
     new_t, grad_self, grad_neigh = pl.pallas_call(
         functools.partial(kernel, doms, feats, owners, slots),
         out_shape=(
@@ -419,23 +466,13 @@
             jax.ShapeDtypeStruct((width, hidden), F32),
             jax.ShapeDtypeStruct((width, hidden), F32),
         ),
-        in_specs=[vmem] * 9,
+        in_specs=[hbm] * 9,
         out_specs=(vmem,) * 3,
         scratch_shapes=scratch,
         compiler_params=pltpu.CompilerParams(
-            collective_id=0, has_side_effects=True, vmem_limit_bytes=40 * 2**20
+            collective_id=0, has_side_effects=True, vmem_limit_bytes=60 * 2**20
         ),
-    )(
-        features,
-        perturb,
-        w_self,
-        w_neigh,
-        bias.reshape(1, hidden),
-        upstream,
-        hub_rows,
-        send_rows,
-        neighbors.T,
-    )
+    )(*args)
     return new_t.T, grad_self, grad_neigh
 
 

time: 36.7 us -> 33.2 us (0.905)
  local copies, waits for them, and re-layouts: 7.77 us -> 3.64 us
  Pallas kernels: 27.9 us -> 28.7 us
    unnamed x21 -> x5, local copies, waits for them, and re-layouts: 7.77 us -> 3.64 us
    pallas_call x1, Pallas kernels: 27.9 us -> 28.7 us  [per_device(): pl.pallas_call(functools.partial(kernel, doms, feats, owners, slots), out...]
where the time goes in v1:
time: 33.2 us; the launch traced here: 33 us
  Pallas kernels  28.7 us (86%)
  local copies, waits for them, and re-layouts  3.64 us (11%)
  between operations  0.64 us (2%)
    pallas_call x1, Pallas kernels, per_device(): pl.pallas_call(functools.partial(kernel, doms, feats, owners, slots), out...  28.7 us
    unnamed x5, local copies, waits for them, and re-layouts  3.64 us

profile of v1, /device:TPU:0, one launch (start us, length us, event | category | flops | bytes accessed | tf_op | source)
XLA Modules:
  0.0 33.0 jit_solution(10252145133315221244)
XLA Ops:
  0.6 28.7 %shard_map.112 = (bf16[32,448]{1,0:T(8,128)(2,1)}, f32[128,256]{1,0:T(8,128)}, f32[128,256]{1,0:T(8,128)}) custom-call(bf16[448,128]{1,0:T(8,128)(2,1)} %features_far.1, bf16[448,128]{1,0:T(8,128)(2,1)} %perturb_far.1, s32[1,4,56]{2,1,0:T(4,128)} %send_rows_far.1, s32[1,2]{1,0:T(1,128)} %hub_rows_far.1, s32[15,448]{1,0:T(8,128)} %bitcast.3, ...), custom_call_target="tpu_custom_call" | custom-call | tf_op jit(solution)/shard_map/pallas_call | solution.py:462
  29.4 1.4 %copy.15 = bf16[448,32]{0,1:T(8,128)(2,1)} copy(bf16[448,32]{0,1:T(8,128)(2,1)} %bitcast.4) | data formatting | bytes 57344
  30.7 0.0 copy-start
  30.7 1.6 %copy.16 = f32[128,256]{1,0:T(8,128)} copy(f32[128,256]{1,0:T(8,128)} %get-tuple-element.13) | data formatting | bytes 262144
  32.4 0.0 copy-done
  32.4 0.7 %copy.17 = f32[128,256]{1,0:T(8,128)} copy(f32[128,256]{1,0:T(8,128)S(1)} %copy-done) | data formatting | bytes 262144
Async XLA Ops:
  30.7 1.6 %copy-start = (f32[128,256]{1,0:T(8,128)S(1)}, f32[128,256]{1,0:T(8,128)}, u32[]{:S(2)}) copy-start(f32[128,256]{1,0:T(8,128)} %get-tuple-element.14) | copy-start | bytes 393220

commit v2 on v1

--- a/solution.py
+++ b/solution.py
@@ -78,6 +78,8 @@
     hubg_in,
     part_out,
     part_in,
+    pair_in,
+    pair_sum,
     whole,
     cols_out,
     cols_in,
@@ -93,6 +95,7 @@
     hubg_r,
     part_s,
     part_r,
+    pair_r,
     whole_s,
     whole_r,
     cols_s,
@@ -298,23 +301,43 @@
         else:
             pl.when(dom < owners)(body)
 
+    flip = 1 - 2 * lax.rem(me, 2)
+    partner = me + flip
+
+    def same(step):
+        return lax.rem(me + 2 * step, doms)
+
+    def pair_send(step):
+        peer = same(step) + flip
+        return copy_to(part_out.at[peer], pair_in.at[peer], part_s.at[peer], pair_r.at[peer], partner, col)
+
+    def pair_recv(step):
+        peer = same(step)
+        return copy_to(part_out.at[peer], pair_in.at[peer], part_s.at[peer], pair_r.at[peer], partner, col)
+
     def part_send(step):
-        peer = dom_peer(step)
-        return copy_to(part_out.at[peer], part_in.at[me], part_s.at[peer], part_r.at[me], peer, col)
+        peer = same(step)
+        return copy_to(pair_sum.at[peer], part_in.at[me], part_s.at[peer], part_r.at[me], peer, col)
 
     def part_recv(step):
-        peer = dom_peer(step)
-        return copy_to(part_out.at[0], part_in.at[peer], part_s.at[peer], part_r.at[peer], peer, col)
+        peer = same(step)
+        return copy_to(pair_sum.at[0], part_in.at[peer], part_s.at[peer], part_r.at[peer], peer, col)
 
     def whole_send(step):
-        peer = dom_peer(step)
+        peer = same(step)
         return copy_to(whole.at[me], whole.at[me], whole_s.at[peer], whole_r.at[me], peer, col)
 
-    def whole_recv(step):
-        peer = dom_peer(step)
+    def whole_recv(peer):
         return copy_to(whole.at[peer], whole.at[peer], whole_s.at[peer], whole_r.at[peer], peer, col)
 
-    each(doms - 1, lambda step: on_owner(dom_peer(step), lambda: part_send(step).start()))
+    def pass_on(step):
+        peer = same(step)
+        return copy_to(
+            whole.at[peer], whole.at[peer], whole_s.at[peer + flip], whole_r.at[peer], partner, col
+        )
+
+    pairs = doms // 2
+    each(pairs, lambda step: on_owner(same(step), lambda: pair_send(step).start()))
 
     local = dot(spread_t, counts[0:rows], NT)
     grad_t = dot(w_self[...], grad_pre, NT) + local[0:width] + local[width:]
@@ -322,6 +345,18 @@
     for o in range(NOFF):
         back_copy(o).wait_recv()
     each(doms - 1, lambda step: hubg_recv(step).wait_recv())
+
+    def add_pair(step):
+        peer = same(step)
+
+        def run():
+            pair_recv(step).wait_recv()
+            pair_sum[peer] = part_out[peer] + pair_in[peer]
+
+        on_owner(peer, run)
+
+    each(pairs, add_pair)
+    each(pairs - 1, lambda step: on_owner(same(step + 1), lambda: part_send(step + 1).start()))
     hubg_in[me] = hubg_out[me]
     hub_sum = jnp.sum(hubg_in[...], 0)
     hub_sum = jnp.concatenate([hub_sum, jnp.zeros((ROW_TILE - HUB_SLOT, width), F32)], 0)
@@ -346,10 +381,13 @@
     each(feats - 1, lambda step: cols_send(step).start())
 
     def sum_parts():
-        each(doms - 1, lambda step: part_recv(step).wait_recv())
-        part_in[me] = part_out[me]
-        whole[me] = jnp.sum(part_in[...], 0)
-        each(doms - 1, lambda step: whole_send(step).start())
+        each(pairs - 1, lambda step: part_recv(step + 1).wait_recv())
+        total = pair_sum[me]
+        for step in range(pairs - 1):
+            total = total + part_in[same(step + 1)]
+        whole[me] = total
+        each(pairs - 1, lambda step: whole_send(step + 1).start())
+        pass_on(0).start()
 
     on_owner(me, sum_parts)
 
@@ -368,6 +406,15 @@
         return copy_to(sq_out, sq_in.at[peer], sq_s.at[peer], sq_r.at[peer], me, peer)
 
     each(feats - 1, lambda step: sq_send(step).start())
+
+    def forward(step):
+        def run():
+            whole_recv(same(step + 1)).wait_recv()
+            pass_on(step + 1).start()
+
+        on_owner(same(step + 1), run)
+
+    each(pairs - 1, forward)
     each(feats - 1, lambda step: sq_recv(step).wait_recv())
     sq_in[col] = sq_out[...]
     mean_square = jnp.sum(sq_in[...], 0)[0:1] / width
@@ -375,9 +422,10 @@
     finish(new_perturb, stepped)
 
     def take_whole(step):
-        on_owner(dom_peer(step), lambda: whole_recv(step).wait_recv())
-
-    each(doms - 1, take_whole)
+        peer = same(step) + flip
+        on_owner(peer, lambda: whole_recv(peer).wait_recv())
+
+    each(pairs, take_whole)
     half = owners // 2
     grad_self[...] = whole[0:half].reshape(grad_self.shape)
     grad_neigh[...] = whole[half:owners].reshape(grad_neigh.shape)
@@ -387,8 +435,10 @@
         back_copy(o).wait_send()
     each(doms - 1, lambda step: hub_send(step).wait_send())
     each(doms - 1, lambda step: hubg_send(step).wait_send())
-    each(doms - 1, lambda step: on_owner(dom_peer(step), lambda: part_send(step).wait_send()))
-    on_owner(me, lambda: each(doms - 1, lambda step: whole_send(step).wait_send()))
+    each(pairs, lambda step: on_owner(same(step), lambda: pair_send(step).wait_send()))
+    each(pairs - 1, lambda step: on_owner(same(step + 1), lambda: part_send(step + 1).wait_send()))
+    on_owner(me, lambda: each(pairs - 1, lambda step: whole_send(step + 1).wait_send()))
+    each(pairs, lambda step: on_owner(same(step), lambda: pass_on(step).wait_send()))
     each(feats - 1, lambda step: cols_send(step).wait_send())
     each(feats - 1, lambda step: sq_send(step).wait_send())
 
@@ -426,6 +476,8 @@
         pltpu.VMEM((owners, chunk, hidden), F32),
         pltpu.VMEM((doms, chunk, hidden), F32),
         pltpu.VMEM((owners, chunk, hidden), F32),
+        pltpu.VMEM((owners, chunk, hidden), F32),
+        pltpu.VMEM((owners, chunk, hidden), F32),
         pltpu.VMEM((feats, part_width, rows), F32),
         pltpu.VMEM((feats, part_width, rows), F32),
         pltpu.VMEM((8, rows), F32),
@@ -436,6 +488,7 @@
         sems((doms,)),
         sems((NOFF,)),
         sems((NOFF,)),
+        sems((doms,)),
         sems((doms,)),
         sems((doms,)),
         sems((doms,)),

time: 33.2 us -> 34.8 us (1.048)
  Pallas kernels: 28.7 us -> 30.3 us
    pallas_call x1, Pallas kernels: 28.7 us -> 30.3 us  [per_device(): pl.pallas_call(functools.partial(kernel, doms, feats, owners, slots), out...]
where the time goes in v2:
time: 34.8 us; the launch traced here: 34.6 us
  Pallas kernels  30.3 us (87%)
  local copies, waits for them, and re-layouts  3.64 us (10%)
  between operations  0.64 us (2%)
    pallas_call x1, Pallas kernels, per_device(): pl.pallas_call(functools.partial(kernel, doms, feats, owners, slots), out...  30.3 us
    unnamed x5, local copies, waits for them, and re-layouts  3.64 us

profile of v2, /device:TPU:0, one launch (start us, length us, event | category | flops | bytes accessed | tf_op | source)
XLA Modules:
  0.0 34.6 jit_solution(11227351563703369974)
XLA Ops:
  0.6 30.3 %shard_map.112 = (bf16[32,448]{1,0:T(8,128)(2,1)}, f32[128,256]{1,0:T(8,128)}, f32[128,256]{1,0:T(8,128)}) custom-call(bf16[448,128]{1,0:T(8,128)(2,1)} %features_far.1, bf16[448,128]{1,0:T(8,128)(2,1)} %perturb_far.1, s32[1,4,56]{2,1,0:T(4,128)} %send_rows_far.1, s32[1,2]{1,0:T(1,128)} %hub_rows_far.1, s32[15,448]{1,0:T(8,128)} %bitcast.3, ...), custom_call_target="tpu_custom_call" | custom-call | tf_op jit(solution)/shard_map/pallas_call | solution.py:515
  30.9 1.4 %copy.15 = bf16[448,32]{0,1:T(8,128)(2,1)} copy(bf16[448,32]{0,1:T(8,128)(2,1)} %bitcast.4) | data formatting | bytes 57344
  32.3 0.0 copy-start
  32.3 1.6 %copy.16 = f32[128,256]{1,0:T(8,128)} copy(f32[128,256]{1,0:T(8,128)} %get-tuple-element.13) | data formatting | bytes 262144
  33.9 0.0 copy-done
  33.9 0.7 %copy.17 = f32[128,256]{1,0:T(8,128)} copy(f32[128,256]{1,0:T(8,128)S(1)} %copy-done) | data formatting | bytes 262144
Async XLA Ops:
  32.3 1.6 %copy-start = (f32[128,256]{1,0:T(8,128)S(1)}, f32[128,256]{1,0:T(8,128)}, u32[]{:S(2)}) copy-start(f32[128,256]{1,0:T(8,128)} %get-tuple-element.14) | copy-start | bytes 393220

commit v3 on v1

--- a/solution.py
+++ b/solution.py
@@ -109,6 +109,8 @@
     w_neigh,
     upstream,
     load_s,
+    new_near,
+    store_s,
 ):
     far = (
         features_far,
@@ -310,10 +312,6 @@
         peer = dom_peer(step)
         return copy_to(whole.at[me], whole.at[me], whole_s.at[peer], whole_r.at[me], peer, col)
 
-    def whole_recv(step):
-        peer = dom_peer(step)
-        return copy_to(whole.at[peer], whole.at[peer], whole_s.at[peer], whole_r.at[peer], peer, col)
-
     each(doms - 1, lambda step: on_owner(dom_peer(step), lambda: part_send(step).start()))
 
     local = dot(spread_t, counts[0:rows], NT)
@@ -372,15 +370,29 @@
     sq_in[col] = sq_out[...]
     mean_square = jnp.sum(sq_in[...], 0)[0:1] / width
     stepped = perturb_t[col] + 0.5 * grad_cols / jnp.sqrt(mean_square + 1e-06)
-    finish(new_perturb, stepped)
-
-    def take_whole(step):
-        on_owner(dom_peer(step), lambda: whole_recv(step).wait_recv())
-
-    each(doms - 1, take_whole)
+    new_near[...] = stepped.astype(BF16)
+    stores = [pltpu.make_async_copy(new_near, new_perturb, store_s.at[owners])]
+    stores[0].start()
+
     half = owners // 2
-    grad_self[...] = whole[0:half].reshape(grad_self.shape)
-    grad_neigh[...] = whole[half:owners].reshape(grad_neigh.shape)
+    for i in range(owners):
+
+        def arrive(i=i):
+            copy_to(
+                whole.at[i], whole.at[i], whole_s.at[i], whole_r.at[i], i, col
+            ).wait_recv()
+
+        pl.when(me != i)(arrive)
+        target = grad_self if i < half else grad_neigh
+        first = i % half * chunk
+        stores.append(
+            pltpu.make_async_copy(
+                whole.at[i], target.at[first : first + chunk], store_s.at[i]
+            )
+        )
+        stores[-1].start()
+    for copy in stores:
+        copy.wait()
 
     for o in range(NOFF):
         halo_copy(o).wait_send()
@@ -391,10 +403,6 @@
     on_owner(me, lambda: each(doms - 1, lambda step: whole_send(step).wait_send()))
     each(feats - 1, lambda step: cols_send(step).wait_send())
     each(feats - 1, lambda step: sq_send(step).wait_send())
-
-
-def finish(new_perturb, stepped):
-    new_perturb[...] = stepped.astype(BF16)
 
 
 def per_device(
@@ -409,7 +417,6 @@
     table = rows + NOFF * slot_pad + doms * HUB_SLOT
     part_width = width // feats
     hbm = pl.BlockSpec(memory_space=pltpu.HBM)
-    vmem = pl.BlockSpec(memory_space=pltpu.VMEM)
     sems = pltpu.SemaphoreType.DMA
     scratch = [
         pltpu.VMEM((8, 128), jnp.int32),
@@ -459,6 +466,7 @@
         upstream,
     )
     scratch += [pltpu.VMEM(x.shape, x.dtype) for x in args] + [sems((len(args),))]
+    scratch += [pltpu.VMEM((part_width, rows), BF16), sems((owners + 1,))]
     new_t, grad_self, grad_neigh = pl.pallas_call(
         functools.partial(kernel, doms, feats, owners, slots),
         out_shape=(
@@ -467,7 +475,7 @@
             jax.ShapeDtypeStruct((width, hidden), F32),
         ),
         in_specs=[hbm] * 9,
-        out_specs=(vmem,) * 3,
+        out_specs=(hbm,) * 3,
         scratch_shapes=scratch,
         compiler_params=pltpu.CompilerParams(
             collective_id=0, has_side_effects=True, vmem_limit_bytes=60 * 2**20

time: 33.2 us -> 33.2 us (level)
  no operation moved by 1% of the time
where the time goes in v3:
time: 33.2 us; the launch traced here: 33 us
  Pallas kernels  28.7 us (86%)
  local copies, waits for them, and re-layouts  3.64 us (11%)
  between operations  0.64 us (2%)
    pallas_call x1, Pallas kernels, per_device(): pl.pallas_call(functools.partial(kernel, doms, feats, owners, slots), out...  28.7 us
    unnamed x5, local copies, waits for them, and re-layouts  3.64 us

profile of v3, /device:TPU:0, one launch (start us, length us, event | category | flops | bytes accessed | tf_op | source)
XLA Modules:
  0.0 33.0 jit_solution(14867989345566361351)
XLA Ops:
  0.6 28.7 %shard_map.112 = (bf16[32,448]{1,0:T(8,128)(2,1)}, f32[128,256]{1,0:T(8,128)}, f32[128,256]{1,0:T(8,128)}) custom-call(bf16[448,128]{1,0:T(8,128)(2,1)} %features_far.1, bf16[448,128]{1,0:T(8,128)(2,1)} %perturb_far.1, s32[1,4,56]{2,1,0:T(4,128)} %send_rows_far.1, s32[1,2]{1,0:T(1,128)} %hub_rows_far.1, s32[15,448]{1,0:T(8,128)} %bitcast.3, ...), custom_call_target="tpu_custom_call" | custom-call | tf_op jit(solution)/shard_map/pallas_call | solution.py:470
  29.3 1.4 %copy.15 = bf16[448,32]{0,1:T(8,128)(2,1)} copy(bf16[448,32]{0,1:T(8,128)(2,1)} %bitcast.4) | data formatting | bytes 57344
  30.7 0.0 copy-start
  30.7 1.6 %copy.16 = f32[128,256]{1,0:T(8,128)} copy(f32[128,256]{1,0:T(8,128)} %get-tuple-element.13) | data formatting | bytes 262144
  32.3 0.0 copy-done
  32.3 0.7 %copy.17 = f32[128,256]{1,0:T(8,128)} copy(f32[128,256]{1,0:T(8,128)S(1)} %copy-done) | data formatting | bytes 262144
Async XLA Ops:
  30.7 1.6 %copy-start = (f32[128,256]{1,0:T(8,128)S(1)}, f32[128,256]{1,0:T(8,128)}, u32[]{:S(2)}) copy-start(f32[128,256]{1,0:T(8,128)} %get-tuple-element.14) | copy-start | bytes 393220
